TPU v7x, 128 devices: a whole 4x4x4 slice. The times are simulated.
128 devices in a mesh: size: 8 (over z, x_lo), gz: 16 (over x_hi, y, core).
Axes of the slice: x: 4 (x_hi: 2, x_lo: 2; x = x_hi * 2 + x_lo), y: 4, z: 4, core: 2. Of those that a mesh axis runs over, the one named last changes fastest.
Arguments:
- tissue: int32 [512, 128, 128], P('gz'), may hold values from 0 to 2
- vessel_pressure: float32 [512, 128, 128], P('gz', 'size'), may hold values from -12 to 12
- cond_table: float32 [3], replicated, may hold values from 0.4 to 1.2
- leak_table: float32 [3], replicated, may hold values from 0.2 to 2
- bind_table: float32 [8, 3], P('size'), may hold values from 0.05 to 1
- hindrance: float32 [8], P('size'), may hold values from 0.2 to 1
- diffusivity: float32 [8], P('size'), may hold values from 0.1 to 0.6
- free_conc: float32 [8, 512, 128, 128], P('size', 'gz'), may hold values from 0 to 2
- bound_conc: float32 [8, 512, 128, 128], P('size', 'gz'), may hold values from 0 to 1
Outputs:
- pressure: float32 [512, 128, 128], P('gz', 'size')
- free_out: float32 [8, 512, 128, 128], P('size', 'gz')
- bound_out: float32 [8, 512, 128, 128], P('size', 'gz')
Inputs may be any that keep to these rules, and one draw needn't show every extreme that they name: 0 marks a vessel cell, 1 necrotic tissue, 2 viable tissue.
All inputs are finite; a program needn't handle non-finite values.
Results may differ from a plain program's by a relative error of at most 0.0001.
Values sent between devices are 32-bit elements; how exact they have to be, the bound alone decides.
A program may use at most 128 MiB of HBM per device.

v0:
```python
import jax
import jax.numpy as jnp
from jax import lax
from jax.sharding import Mesh
from jax.sharding import PartitionSpec as P

ITERS = 2
TSTEPS = 2
SIZE_GZ = ("size_0", "size_1", "gz_0", "gz_1", "gz_2")
SIZE = ("size_0", "size_1")
GZ = ("gz_0", "gz_1", "gz_2")
time_step = 0.1


def extended(array, sides, width):
    edges = {}
    for axis, dim in sides:
        peers, length = (lax.axis_size(axis), array.shape[dim])
        up = [(i, (i + 1) % peers) for i in range(peers - 1)]
        last = lax.slice_in_dim(array, length - width, length, axis=dim)
        initial = lax.slice_in_dim(array, 0, width, axis=dim)
        edges[dim] = (
            lax.ppermute(last, axis, up),
            lax.ppermute(initial, axis, [(b, a) for a, b in up]),
        )
    done = []
    for _, dim in sides:
        low, high = edges[dim]
        around = [(width, width) if d in done else (0, 0) for d in range(array.ndim)]
        array = jnp.concatenate([jnp.pad(low, around), array, jnp.pad(high, around)], axis=dim)
        done.append(dim)
    return array


def by_axis(array, axes):
    for axis in axes:
        array = lax.psum(array, axis)
    return array


def from_everyone(array, axis):
    copies = jnp.broadcast_to(array, (lax.axis_size(axis), *array.shape))
    return lax.all_to_all(copies, axis, split_axis=0, concat_axis=0, tiled=True)


def in_order(blocks, dim):
    lengths = list(blocks.shape[1:])
    lengths[dim] *= blocks.shape[0]
    return jnp.moveaxis(blocks, 0, dim).reshape(lengths)


def gathered_copies(array, axis, dim):
    blocks = from_everyone(array, axis)
    return in_order(blocks, dim)


def extended_2(cells, sides, width):
    for axis, dim in sides:
        count = lax.axis_size(axis)
        ends = count - 1
        head = lax.slice_in_dim(cells, 0, width, axis=dim)
        tail = lax.slice_in_dim(cells, cells.shape[dim] - width, cells.shape[dim], axis=dim)
        cells = jnp.concatenate(
            [
                lax.ppermute(tail, axis, [(i, (i + 1) % count) for i in range(ends)]),
                cells,
                lax.ppermute(head, axis, [((i + 1) % count, i) for i in range(ends)]),
            ],
            axis=dim,
        )
    return cells


def lookup(table, labels):
    return jnp.where(labels == 0, table[0], jnp.where(labels == 1, table[1], table[2]))


def neighbours(padded):
    total = padded[2:, 1:-1, 1:-1] + padded[:-2, 1:-1, 1:-1]
    total = total + padded[1:-1, 2:, 1:-1] + padded[1:-1, :-2, 1:-1]
    total = total + padded[1:-1, 1:-1, 2:] + padded[1:-1, 1:-1, :-2]
    return total


def apply_operator(vector, conduct, leak):
    scaled = conduct * vector
    rimmed = extended(scaled, ((SIZE, 1), (GZ, 0)), 1)
    padded = jnp.pad(rimmed, ((0, 0), (0, 0), (1, 1)))
    return conduct * (6.0 * scaled - neighbours(padded)) + leak * vector


def paired_products(residual, precond, image):
    return (
        by_axis(jnp.sum(residual * precond), SIZE_GZ),
        by_axis(jnp.sum(precond * image), SIZE_GZ),
    )


def along_line(array, along_dim):
    return array[tuple((slice(None) if k == along_dim else slice(1, -1) for k in range(3)))]


def lower_part(array, along_dim):
    return array[tuple((slice(0, -1) if k == along_dim else slice(None) for k in range(3)))]


def upper_part(array, along_dim):
    return array[tuple((slice(1, None) if k == along_dim else slice(None) for k in range(3)))]


def transport_step(conc_pad, fields_pad, hinder, diffuse):
    divergence = None
    for along_dim in range(3):
        conc_line = along_line(conc_pad, along_dim)
        press_line = along_line(fields_pad[0], along_dim)
        cond_line = along_line(fields_pad[1], along_dim)
        conc_low = lower_part(conc_line, along_dim)
        conc_high = upper_part(conc_line, along_dim)
        velocity = (
            hinder
            * lower_part(cond_line, along_dim)
            * upper_part(cond_line, along_dim)
            * (lower_part(press_line, along_dim) - upper_part(press_line, along_dim))
        )
        flux = (
            jnp.maximum(velocity, 0.0) * conc_low
            + jnp.minimum(velocity, 0.0) * conc_high
            + diffuse * (conc_low - conc_high)
        )
        term = upper_part(flux, along_dim) - lower_part(flux, along_dim)
        divergence = term if divergence is None else divergence + term
    conc = conc_pad[1:-1, 1:-1, 1:-1]
    rate = fields_pad[2][1:-1, 1:-1, 1:-1]
    bind = rate * conc
    return (conc - time_step * (divergence + bind), bind)


def pad_plane(array):
    return jnp.pad(array, ((0, 0), (1, 1), (1, 1)))


def local(
    tissue,
    vessel_pressure,
    cond_table,
    leak_table,
    bind_table,
    hindrance,
    diffusivity,
    free_conc,
    bound_conc,
):
    block_x = vessel_pressure.shape[1]
    slab_z = vessel_pressure.shape[0]
    local_tissue = lax.dynamic_slice_in_dim(tissue, lax.axis_index(SIZE) * block_x, block_x, 1)
    conduct = lookup(cond_table, local_tissue)
    leak = lookup(leak_table, local_tissue)
    diag = 6.0 * conduct * conduct + leak
    source = leak * vessel_pressure
    solution = jnp.zeros_like(source)
    residual = source
    precond = residual / diag
    image = apply_operator(precond, conduct, leak)
    rho_now, product = paired_products(residual, precond, image)
    alpha = rho_now / product
    direction = precond
    along_image = image
    for iteration in range(ITERS):
        solution = solution + alpha * direction
        residual = residual - alpha * along_image
        if iteration + 1 < ITERS:
            precond = residual / diag
            image = apply_operator(precond, conduct, leak)
            rho_next, product = paired_products(residual, precond, image)
            ratio = rho_next / rho_now
            alpha = rho_next / (product - ratio * rho_next / alpha)
            direction = precond + ratio * direction
            along_image = image + ratio * along_image
            rho_now = rho_next
    conduct_slab = lookup(cond_table, tissue)
    rate_slab = lookup(bind_table[0], tissue)
    slab_pressure = gathered_copies(solution, SIZE, 1)
    stacked = jnp.stack([slab_pressure, conduct_slab, rate_slab])
    rimmed = extended_2(stacked, ((GZ, 1),), TSTEPS)
    fields_pad = jnp.pad(rimmed, ((0, 0), (0, 0), (1, 1), (1, 1)))
    hinder = hindrance[0]
    diffuse = diffusivity[0]
    conc = free_conc[0]
    bound = bound_conc[0]
    fields_one = fields_pad[:, TSTEPS - 1 : TSTEPS + 1 + slab_z]
    for sweep in range(TSTEPS):
        conc_pad = pad_plane(extended_2(conc, ((GZ, 0),), 1))
        conc, bind = transport_step(conc_pad, fields_one, hinder, diffuse)
        bound = bound + time_step * bind
    return (solution, conc[None], bound[None])


def solution(mesh):
    finer = Mesh(mesh.devices.reshape(4, 2, 2, 4, 2), ("size_0", "size_1", "gz_0", "gz_1", "gz_2"))
    return jax.shard_map(
        local,
        mesh=finer,
        in_specs=(
            P(GZ, None, None),
            P(GZ, SIZE, None),
            P(),
            P(),
            P(SIZE, None),
            P(SIZE),
            P(SIZE),
            P(SIZE, GZ, None, None),
            P(SIZE, GZ, None, None),
        ),
        out_specs=(P(GZ, SIZE, None), P(SIZE, GZ, None, None), P(SIZE, GZ, None, None)),
        check_vma=False,
    )
```

profile of v0, /device:TPU:6, one launch (start us, length us, event | category | flops | bytes accessed | tf_op | source)
XLA Modules:
  0.0 285.2 jit_solution(7565283562360594348)
XLA Ops:
  3.4 5.1 %fusion.39 = (f32[32,16,128]{2,1,0:T(8,128)S(1)}, pred[32,16,128]{2,1,0:T(8,128)(4,1)S(1)}, pred[32,16,128]{2,1,0:T(8,128)(4,1)S(1)}) fusion(f32[]{:T(128)} %bitcast.5, f32[]{:T(128)} %bitcast.4, f32[]{:T(128)} %bitcast.3, f32[32,16,128]{2,1,0:T(8,128)} %param.10, f32[]{:T(128)} %bitcast.2, f32[]{:T(128)} %bitcast.1, f32[]{:T(128)} %bitcast, ...), kind=kLoop, calls=%fused_computation.130 | loop fusion | flops 786432 | bytes 917532 | tf_op jit(solution)/shard_map/mul | solution.py:86
  8.5 2.7 collective-permute-start.1
  11.3 4.0 %collective-permute-start = (f32[32,1,128]{2,1,0:T(1,128)S(1)}, f32[32,1,128]{2,1,0:T(1,128)S(1)}, u32[]{:S(2)}, u32[]{:S(2)}) collective-permute-start(f32[32,1,128]{2,1,0:T(1,128)S(1)} %get-tuple-element.55), channel_id=1, source_target_pairs={{0,16},{16,32},{32,48},{48,64},{64,80},{80,96},{96,112},{1,17},{17... | collective-permute-start | bytes 49160 | tf_op jit(solution)/shard_map/ppermute | solution.py:23
  15.3 4.6 %collective-permute-start.2 = (f32[1,16,128]{2,1,0:T(8,128)S(1)}, f32[1,16,128]{2,1,0:T(8,128)S(1)}, u32[]{:S(2)}, u32[]{:S(2)}) collective-permute-start(f32[1,16,128]{2,1,0:T(8,128)S(1)} %get-tuple-element.58), channel_id=1, source_target_pairs={{1,0},{2,1},{3,2},{4,3},{5,4},{6,5},{7,6},{8,7},{9,8},{10,9},{11,1... | collective-permute-start | bytes 24584 | tf_op jit(solution)/shard_map/ppermute | solution.py:24
  19.9 1.9 collective-permute-start.3
  21.9 6.6 %collective-permute-done.3 = f32[1,16,128]{2,1,0:T(8,128)S(1)} collective-permute-done((f32[1,16,128]{2,1,0:T(8,128)S(1)}, f32[1,16,128]{2,1,0:T(8,128)S(1)}, u32[]{:S(2)}, u32[]{:S(2)}) %collective-permute-start.3) | collective-permute-done | bytes 8224 | tf_op jit(solution)/shard_map/ppermute | solution.py:23
  29.0 4.9 %multiply_reduce_fusion.1 = (f32[]{:T(128)}, f32[]{:T(128)}, f32[32,16,128]{2,1,0:T(8,128)S(1)}) fusion(pred[32,16,128]{2,1,0:T(8,128)(4,1)S(1)} %get-tuple-element.39, pred[32,16,128]{2,1,0:T(8,128)(4,1)S(1)} %get-tuple-element.38, f32[]{:T(128)} %bitcast.5, f32[]{:T(128)} %bitcast.4, f32[]{:T(128)} %bitcast.3, f32[32,16,128]{2,1,0:T(8,128)S(1)} %copy-done.6, ...), kind=kLoop, calls=%fused_computation.126 | loop fusion | flops 2031614 | bytes 1493024 | tf_op jit(solution)/shard_map/reduce_sum | solution.py:95
  33.9 10.3 %all-reduce.12 = (f32[]{:T(128)}, f32[]{:T(128)}) all-reduce(f32[]{:T(128)} %get-tuple-element.4, f32[]{:T(128)} %get-tuple-element.3), channel_id=1, replica_groups=mesh['size_0'=4,'size_1'=2,'gz_0'=2,'gz_1'=4,'gz_2'=2] {'size_0'}, use_global_device_ids=true, to_apply=%region_1.2 | all-reduce | flops 2 | bytes 16 | tf_op jit(solution)/shard_map/psum | solution.py:37
  44.2 5.6 %all-reduce.18 = (f32[]{:T(128)}, f32[]{:T(128)}) all-reduce(f32[]{:T(128)} %get-tuple-element.11, f32[]{:T(128)} %get-tuple-element.12), channel_id=1, replica_groups=mesh['size_0'=4,'size_1'=2,'gz_0'=2,'gz_1'=4,'gz_2'=2] {'size_1'}, use_global_device_ids=true, to_apply=%region_2.3 | all-reduce | flops 2 | bytes 16 | tf_op jit(solution)/shard_map/psum | solution.py:37
  49.9 7.1 %all-reduce.16 = (f32[]{:T(128)}, f32[]{:T(128)}) all-reduce(f32[]{:T(128)} %get-tuple-element.23, f32[]{:T(128)} %get-tuple-element.24), channel_id=1, replica_groups=mesh['size_0'=4,'size_1'=2,'gz_0'=2,'gz_1'=4,'gz_2'=2] {'gz_0'}, use_global_device_ids=true, to_apply=%region_3.4 | all-reduce | flops 2 | bytes 16 | tf_op jit(solution)/shard_map/psum | solution.py:37
  57.0 8.4 %all-reduce.10 = (f32[]{:T(128)}, f32[]{:T(128)}) all-reduce(f32[]{:T(128)} %get-tuple-element.19, f32[]{:T(128)} %get-tuple-element.20), channel_id=1, replica_groups=mesh['size_0'=4,'size_1'=2,'gz_0'=2,'gz_1'=4,'gz_2'=2] {'gz_1'}, use_global_device_ids=true, to_apply=%region_4.5 | all-reduce | flops 2 | bytes 16 | tf_op jit(solution)/shard_map/psum | solution.py:37
  65.5 3.2 %all-reduce.14 = (f32[]{:T(128)}, f32[]{:T(128)}) all-reduce(f32[]{:T(128)} %get-tuple-element.7, f32[]{:T(128)} %get-tuple-element.8), channel_id=1, replica_groups=mesh['size_0'=4,'size_1'=2,'gz_0'=2,'gz_1'=4,'gz_2'=2] {'gz_2'}, use_global_device_ids=true, to_apply=%region_5.6 | all-reduce | flops 2 | bytes 16 | tf_op jit(solution)/shard_map/psum | solution.py:37
  69.9 4.7 %fusion.38 = (f32[32,16,128]{2,1,0:T(8,128)S(1)}, f32[]{:T(128)}) fusion(pred[32,16,128]{2,1,0:T(8,128)(4,1)S(1)} %get-tuple-element.39, pred[32,16,128]{2,1,0:T(8,128)(4,1)S(1)} %get-tuple-element.38, f32[]{:T(128)} %bitcast.5, f32[]{:T(128)} %bitcast.4, f32[]{:T(128)} %bitcast.3, f32[32,16,128]{2,1,0:T(8,128)S(1)} %get-tuple-element.36, f32[]{:T(128)S(6)} %div.19, ...), kind=kLoop, calls=%fused_computation.129 | loop fusion | flops 917503 | bytes 917536 | tf_op jit(solution)/shard_map/mul | solution.py:86
  74.7 3.0 %collective-permute-start.5 = (f32[32,1,128]{2,1,0:T(1,128)S(1)}, f32[32,1,128]{2,1,0:T(1,128)S(1)}, u32[]{:S(2)}, u32[]{:S(2)}) collective-permute-start(f32[32,1,128]{2,1,0:T(1,128)S(1)} %get-tuple-element.52), channel_id=1, source_target_pairs={{16,0},{32,16},{48,32},{64,48},{80,64},{96,80},{112,96},{17,1},{33... | collective-permute-start | bytes 49160 | tf_op jit(solution)/shard_map/ppermute | solution.py:24
  77.7 3.7 %collective-permute-start.4 = (f32[32,1,128]{2,1,0:T(1,128)S(1)}, f32[32,1,128]{2,1,0:T(1,128)S(1)}, u32[]{:S(2)}, u32[]{:S(2)}) collective-permute-start(f32[32,1,128]{2,1,0:T(1,128)S(1)} %get-tuple-element.51), channel_id=1, source_target_pairs={{0,16},{16,32},{32,48},{48,64},{64,80},{80,96},{96,112},{1,17},{17... | collective-permute-start | bytes 49160 | tf_op jit(solution)/shard_map/ppermute | solution.py:23
  81.4 2.5 collective-permute-start.6
  84.0 1.9 collective-permute-start.7
  85.9 6.6 %collective-permute-done.7 = f32[1,16,128]{2,1,0:T(8,128)S(1)} collective-permute-done((f32[1,16,128]{2,1,0:T(8,128)S(1)}, f32[1,16,128]{2,1,0:T(8,128)S(1)}, u32[]{:S(2)}, u32[]{:S(2)}) %collective-permute-start.7) | collective-permute-done | bytes 8224 | tf_op jit(solution)/shard_map/ppermute | solution.py:23
  93.0 4.9 %fusion.28 = f32[]{:T(128)} fusion(f32[34,18,130]{2,1,0:T(8,128)S(1)} %select_maximum_fusion.8, f32[32,16,128]{2,1,0:T(8,128)S(1)} %get-tuple-element.49, f32[32,1,128]{2,1,0:T(1,128)S(1)} %collective-permute-done.4, f32[32,1,128]{2,1,0:T(1,128)S(1)} %collective-permute-done.5, f32[1,18,128]{2,1,0:T(8,128)S(1)} %pad.35, f32[1,18,128]{2,1,0:T(8,128)S(1)} %pad.34, ...), kind=kLoop, calls=%fused_computation.94 | loop fusion | flops 2031615 | bytes 1493024 | tf_op jit(solution)/shard_map/reduce_sum | solution.py:95
  97.9 9.7 %all-reduce.11 = (f32[]{:T(128)}, f32[]{:T(128)}) all-reduce(f32[]{:T(128)} %get-tuple-element.50, f32[]{:T(128)} %fusion.28), channel_id=1, replica_groups=mesh['size_0'=4,'size_1'=2,'gz_0'=2,'gz_1'=4,'gz_2'=2] {'size_0'}, use_global_device_ids=true, to_apply=%region_13.14 | all-reduce | flops 2 | bytes 16 | tf_op jit(solution)/shard_map/psum | solution.py:37
  107.6 5.6 %all-reduce.17 = (f32[]{:T(128)}, f32[]{:T(128)}) all-reduce(f32[]{:T(128)} %get-tuple-element.9, f32[]{:T(128)} %get-tuple-element.10), channel_id=1, replica_groups=mesh['size_0'=4,'size_1'=2,'gz_0'=2,'gz_1'=4,'gz_2'=2] {'size_1'}, use_global_device_ids=true, to_apply=%region_14.15 | all-reduce | flops 2 | bytes 16 | tf_op jit(solution)/shard_map/psum | solution.py:37
  113.2 7.1 %all-reduce.15 = (f32[]{:T(128)}, f32[]{:T(128)}) all-reduce(f32[]{:T(128)} %get-tuple-element.21, f32[]{:T(128)} %get-tuple-element.22), channel_id=1, replica_groups=mesh['size_0'=4,'size_1'=2,'gz_0'=2,'gz_1'=4,'gz_2'=2] {'gz_0'}, use_global_device_ids=true, to_apply=%region_15.16 | all-reduce | flops 2 | bytes 16 | tf_op jit(solution)/shard_map/psum | solution.py:37
  120.4 8.4 %all-reduce.9 = (f32[]{:T(128)}, f32[]{:T(128)}) all-reduce(f32[]{:T(128)} %get-tuple-element.17, f32[]{:T(128)} %get-tuple-element.18), channel_id=1, replica_groups=mesh['size_0'=4,'size_1'=2,'gz_0'=2,'gz_1'=4,'gz_2'=2] {'gz_1'}, use_global_device_ids=true, to_apply=%region_16.17 | all-reduce | flops 2 | bytes 16 | tf_op jit(solution)/shard_map/psum | solution.py:37
  128.8 3.1 %all-reduce.13 = (f32[]{:T(128)}, f32[]{:T(128)}) all-reduce(f32[]{:T(128)} %get-tuple-element.5, f32[]{:T(128)} %get-tuple-element.6), channel_id=1, replica_groups=mesh['size_0'=4,'size_1'=2,'gz_0'=2,'gz_1'=4,'gz_2'=2] {'gz_2'}, use_global_device_ids=true, to_apply=%region_17.18 | all-reduce | flops 2 | bytes 16 | tf_op jit(solution)/shard_map/psum | solution.py:37
  136.6 4.1 %multiply_add_fusion.6 = f32[32,16,128]{2,1,0:T(8,128)S(1)} fusion(f32[]{:T(128)S(6)} %div.21, f32[]{:T(128)S(6)} %div.23, f32[]{:T(128)S(6)} %div.19, pred[32,16,128]{2,1,0:T(8,128)(4,1)S(1)} %get-tuple-element.39, pred[32,16,128]{2,1,0:T(8,128)(4,1)S(1)} %get-tuple-element.38, f32[]{:T(128)} %bitcast.5, f32[]{:T(128)} %bitcast.4, f32[]{:T(128)} %bitcast.3, ...), kind=kLoop, calls=%fused_computation.123 | loop fusion | flops 1114112 | bytes 917540 | tf_op jit(solution)/shard_map/add | solution.py:169
  142.2 4.4 %all-to-all-start = ((f32[8,32,16,128]{3,2,1,0:T(8,128)}), f32[8,32,16,128]{3,2,1,0:T(8,128)}, u32[]{:S(2)}, u32[]{:S(2)}) async-start(f32[8,32,16,128]{3,2,1,0:T(8,128)} %broadcast_in_dim.57), calls=%async_computation | async-start | bytes 4194304 | tf_op jit(solution)/shard_map/all_to_all | solution.py:43
  146.6 3.3 %collective-permute-start.11 = (f32[1,128,128]{2,1,0:T(8,128)S(1)}, f32[1,128,128]{2,1,0:T(8,128)S(1)}, u32[]{:S(2)}, u32[]{:S(2)}) collective-permute-start(f32[1,128,128]{2,1,0:T(8,128)S(1)} %get-tuple-element.48), channel_id=1, source_target_pairs={{1,0},{2,1},{3,2},{4,3},{5,4},{6,5},{7,6},{8,7},{9,8},{10,9},{11,1... | collective-permute-start | bytes 196616 | tf_op jit(solution)/shard_map/ppermute | solution.py:67
  150.0 1.9 collective-permute-start.10
  153.9 5.6 %select_bitcast_fusion.1 = (f32[1,32,128,128]{3,2,1,0:T(8,128)}, pred[32,128,128]{2,1,0:T(8,128)(4,1)S(1)}, pred[32,128,128]{2,1,0:T(8,128)(4,1)S(1)}) fusion(f32[]{:T(128)} %bitcast.5, f32[]{:T(128)} %bitcast.4, f32[]{:T(128)} %bitcast.3, s32[32,128,128]{2,1,0:T(8,128)} %param.9), kind=kLoop, calls=%fused_computation.68 | loop fusion | flops 2097152 | bytes 5242892 | tf_op jit(solution)/shard_map/stack | solution.py:183
  159.4 3.6 %select_bitcast_fusion = f32[1,32,128,128]{3,2,1,0:T(8,128)} fusion(pred[32,128,128]{2,1,0:T(8,128)(4,1)S(1)} %get-tuple-element.35, pred[32,128,128]{2,1,0:T(8,128)(4,1)S(1)} %get-tuple-element.34, f32[]{:T(128)} %bitcast.13, f32[]{:T(128)} %bitcast.12, f32[]{:T(128)} %bitcast.11), kind=kLoop, calls=%fused_computation.67 | loop fusion | flops 1048576 | bytes 3145740 | tf_op jit(solution)/shard_map/stack | solution.py:183
  163.1 10.0 %all-to-all-done = f32[8,32,16,128]{3,2,1,0:T(8,128)} async-done(((f32[8,32,16,128]{3,2,1,0:T(8,128)}), f32[8,32,16,128]{3,2,1,0:T(8,128)}, u32[]{:S(2)}, u32[]{:S(2)}) %all-to-all-start) | async-done | bytes 2097184 | tf_op jit(solution)/shard_map/all_to_all | solution.py:43
  173.0 2.0 copy.12
  175.9 2.9 %collective-permute-start.9 = (f32[3,2,128,128]{3,2,1,0:T(8,128)S(1)}, f32[3,2,128,128]{3,2,1,0:T(8,128)S(1)}, u32[]{:S(2)}, u32[]{:S(2)}) collective-permute-start(f32[3,2,128,128]{3,2,1,0:T(8,128)S(1)} %get-tuple-element.44), channel_id=1, source_target_pairs={{1,0},{2,1},{3,2},{4,3},{5,4},{6,5},{7,6},{8,7},{9,8},{10,9},{11,1... | collective-permute-start | bytes 1179656 | tf_op jit(solution)/shard_map/ppermute | solution.py:67
  178.8 2.1 collective-permute-start.8
  181.0 4.3 %select_maximum_fusion.6 = f32[34,130,130]{2,1,0:T(8,128)} fusion(f32[1,128,128]{2,1,0:T(8,128)S(1)} %collective-permute-done.11, f32[32,128,128]{2,1,0:T(8,128)S(1)} %bitcast.57, f32[1,128,128]{2,1,0:T(8,128)S(1)} %collective-permute-done.10), kind=kLoop, calls=%fused_computation.18 | loop fusion | flops 8619000 | bytes 4526624 | tf_op jit(solution)/shard_map/concatenate | solution.py:63
  185.3 6.3 %collective-permute-done.8 = f32[3,2,128,128]{3,2,1,0:T(8,128)S(1)} collective-permute-done((f32[3,2,128,128]{3,2,1,0:T(8,128)S(1)}, f32[3,2,128,128]{3,2,1,0:T(8,128)S(1)}, u32[]{:S(2)}, u32[]{:S(2)}) %collective-permute-start.8) | collective-permute-done | bytes 393248 | tf_op jit(solution)/shard_map/ppermute | solution.py:65
  191.5 15.3 %select_maximum_fusion = f32[3,36,130,130]{3,2,1,0:T(8,128)} fusion(f32[3,2,128,128]{3,2,1,0:T(8,128)S(1)} %collective-permute-done.9, f32[3,2,128,128]{3,2,1,0:T(8,128)S(1)} %collective-permute-done.8, f32[1,32,128,128]{3,2,1,0:T(8,128)S(1)} %copy-done.2, f32[1,32,128,128]{3,2,1,0:T(8,128)S(1)} %copy-done.1, f32[1,32,128,128]{3,2,1,0:T(8,128)S(1)} %bitcast.60), kind=kLoop, calls=%fused_computation.4 | loop fusion | flops 38329200 | bytes 14378688 | tf_op jit(solution)/shard_map/concatenate | solution.py:63
  206.8 10.4 %slice_bitcast_fusion.2 = (f32[34,130,130]{2,1,0:T(8,128)}, f32[34,130,130]{2,1,0:T(8,128)}, f32[34,130,130]{2,1,0:T(8,128)}) fusion(f32[3,36,130,130]{3,2,1,0:T(8,128)} %select_maximum_fusion), kind=kLoop, calls=%fused_computation.21 | loop fusion | bytes 13790400 | tf_op jit(solution)/shard_map/squeeze | solution.py:116
  217.3 15.7 %multiply_add_fusion.1 = (f32[32,128,129]{2,1,0:T(8,128)}, f32[32,128,129]{2,1,0:T(8,128)}) fusion(f32[34,130,130]{2,1,0:T(8,128)} %select_maximum_fusion.6, f32[]{:T(128)} %bitcast.47, f32[34,130,130]{2,1,0:T(8,128)} %get-tuple-element.41, f32[34,130,130]{2,1,0:T(8,128)} %get-tuple-element.40, f32[]{:T(128)} %bitcast.44), kind=kLoop, calls=%fused_computation.30 | loop fusion | flops 6340608 | bytes 16908296 | tf_op jit(solution)/shard_map/add | solution.py:126
  233.0 5.0 %multiply_add_fusion.3 = (f32[32,129,128]{2,1,0:T(8,128)}, f32[32,129,128]{2,1,0:T(8,128)}) fusion(f32[34,130,130]{2,1,0:T(8,128)S(1)} %bitcast.56, f32[]{:T(128)} %bitcast.46, f32[34,130,130]{2,1,0:T(8,128)S(1)} %bitcast.54, f32[34,130,130]{2,1,0:T(8,128)S(1)} %bitcast.52, f32[]{:T(128)} %bitcast.43), kind=kLoop, calls=%fused_computation.36 | loop fusion | flops 6340608 | bytes 16908296 | tf_op jit(solution)/shard_map/add | solution.py:126
  238.1 9.3 %multiply_add_fusion.5 = (f32[33,128,128]{2,1,0:T(8,128)}, f32[33,128,128]{2,1,0:T(8,128)}) fusion(f32[1,128,128]{2,1,0:T(8,128)S(1)} %collective-permute-done.11, f32[32,128,128]{2,1,0:T(8,128)S(1)} %bitcast.58, f32[1,128,128]{2,1,0:T(8,128)S(1)} %collective-permute-done.10, f32[]{:T(128)} %bitcast.45, f32[34,130,130]{2,1,0:T(8,128)} %get-tuple-element.41, ...), kind=kLoop, calls=%fused_computation.46 | loop fusion | flops 7569408 | bytes 15204360 | tf_op jit(solution)/shard_map/add | solution.py:126
  247.4 9.7 %fusion.21 = (f32[1,32,128,128]{3,2,1,0:T(8,128)}, f32[32,128,128]{2,1,0:T(8,128)S(1)}) fusion(f32[1,32,128,128]{3,2,1,0:T(8,128)} %param.17, f32[34,130,130]{2,1,0:T(8,128)} %get-tuple-element.42, f32[1,32,128,128]{3,2,1,0:T(8,128)S(1)} %copy-done, f32[32,128,129]{2,1,0:T(8,128)} %get-tuple-element.31, f32[32,129,128]{2,1,0:T(8,128)} %get-tuple-element.29, ...), kind=kLoop, calls=%fused_computation.66 | loop fusion | flops 7340032 | bytes 23068672 | tf_op jit(solution)/shard_map/broadcast_in_dim | solution.py:195
  257.1 1.9 collective-permute-start.13
  259.0 2.9 %collective-permute-start.12 = (f32[1,128,128]{2,1,0:T(8,128)S(1)}, f32[1,128,128]{2,1,0:T(8,128)S(1)}, u32[]{:S(2)}, u32[]{:S(2)}) collective-permute-start(f32[1,128,128]{2,1,0:T(8,128)S(1)} %get-tuple-element.45), channel_id=1, source_target_pairs={{0,1},{1,2},{2,3},{3,4},{4,5},{5,6},{6,7},{7,8},{8,9},{9,10},{10,1... | collective-permute-start | bytes 196616 | tf_op jit(solution)/shard_map/ppermute | solution.py:65
  261.9 6.6 %collective-permute-done.12 = f32[1,128,128]{2,1,0:T(8,128)S(1)} collective-permute-done((f32[1,128,128]{2,1,0:T(8,128)S(1)}, f32[1,128,128]{2,1,0:T(8,128)S(1)}, u32[]{:S(2)}, u32[]{:S(2)}) %collective-permute-start.12) | collective-permute-done | bytes 65568 | tf_op jit(solution)/shard_map/ppermute | solution.py:65
  268.5 2.9 %select_maximum_fusion.4 = f32[34,130,130]{2,1,0:T(8,128)S(1)} fusion(f32[1,128,128]{2,1,0:T(8,128)S(1)} %collective-permute-done.13, f32[32,128,128]{2,1,0:T(8,128)S(1)} %get-tuple-element.26, f32[1,128,128]{2,1,0:T(8,128)S(1)} %collective-permute-done.12), kind=kLoop, calls=%fused_computation.15 | loop fusion | flops 8619000 | bytes 4526624 | tf_op jit(solution)/shard_map/concatenate | solution.py:63
  271.4 4.2 %multiply_add_fusion = f32[32,128,129]{2,1,0:T(8,128)} fusion(f32[34,130,130]{2,1,0:T(8,128)S(1)} %select_maximum_fusion.4, f32[32,128,129]{2,1,0:T(8,128)S(1)} %copy-done.3, f32[]{:T(128)} %bitcast.48), kind=kLoop, calls=%fused_computation.29 | loop fusion | flops 4227072 | bytes 8454148 | tf_op jit(solution)/shard_map/add | solution.py:126
  277.9 7.3 %fusion.13 = f32[1,32,128,128]{3,2,1,0:T(8,128)} fusion(f32[32,128,128]{2,1,0:T(8,128)S(1)} %get-tuple-element.26, f32[32,128,129]{2,1,0:T(8,128)} %multiply_add_fusion, f32[32,129,128]{2,1,0:T(8,128)S(1)} %multiply_add_fusion.2, f32[33,128,128]{2,1,0:T(8,128)S(1)} %multiply_add_fusion.4, f32[34,130,130]{2,1,0:T(8,128)} %get-tuple-element.42), kind=kLoop, calls=%fused_computation.52 | loop fusion | flops 4718592 | bytes 18874368 | tf_op jit(solution)/shard_map/broadcast_in_dim | solution.py:195
  (62 shorter events, 9.1 us)
Async XLA Ops:
  0.6 28.3 %copy-start.6 = (f32[32,16,128]{2,1,0:T(8,128)S(1)}, f32[32,16,128]{2,1,0:T(8,128)}, u32[]{:S(2)}) copy-start(f32[32,16,128]{2,1,0:T(8,128)} %param.10) | copy-start | bytes 786436
  8.5 20.0 %collective-permute-start.1 = (f32[32,1,128]{2,1,0:T(1,128)S(1)}, f32[32,1,128]{2,1,0:T(1,128)S(1)}, u32[]{:S(2)}, u32[]{:S(2)}) collective-permute-start(f32[32,1,128]{2,1,0:T(1,128)S(1)} %get-tuple-element.56), channel_id=1, source_target_pairs={{16,0},{32,16},{48,32},{64,48},{80,64},{96,80},{112,96},{17,1},{33... | collective-permute-start | bytes 49160 | tf_op jit(solution)/shard_map/ppermute | solution.py:24
  11.3 17.3 %collective-permute-start = (f32[32,1,128]{2,1,0:T(1,128)S(1)}, f32[32,1,128]{2,1,0:T(1,128)S(1)}, u32[]{:S(2)}, u32[]{:S(2)}) collective-permute-start(f32[32,1,128]{2,1,0:T(1,128)S(1)} %get-tuple-element.55), channel_id=1, source_target_pairs={{0,16},{16,32},{32,48},{48,64},{64,80},{80,96},{96,112},{1,17},{17... | collective-permute-start | bytes 49160 | tf_op jit(solution)/shard_map/ppermute | solution.py:23
  15.3 6.6 %collective-permute-start.2 = (f32[1,16,128]{2,1,0:T(8,128)S(1)}, f32[1,16,128]{2,1,0:T(8,128)S(1)}, u32[]{:S(2)}, u32[]{:S(2)}) collective-permute-start(f32[1,16,128]{2,1,0:T(8,128)S(1)} %get-tuple-element.58), channel_id=1, source_target_pairs={{1,0},{2,1},{3,2},{4,3},{5,4},{6,5},{7,6},{8,7},{9,8},{10,9},{11,1... | collective-permute-start | bytes 24584 | tf_op jit(solution)/shard_map/ppermute | solution.py:24
  19.9 8.6 %collective-permute-start.3 = (f32[1,16,128]{2,1,0:T(8,128)S(1)}, f32[1,16,128]{2,1,0:T(8,128)S(1)}, u32[]{:S(2)}, u32[]{:S(2)}) collective-permute-start(f32[1,16,128]{2,1,0:T(8,128)S(1)} %get-tuple-element.57), channel_id=1, source_target_pairs={{0,1},{1,2},{2,3},{3,4},{4,5},{5,6},{6,7},{7,8},{8,9},{9,10},{10,1... | collective-permute-start | bytes 24584 | tf_op jit(solution)/shard_map/ppermute | solution.py:23
  74.7 17.9 %collective-permute-start.5 = (f32[32,1,128]{2,1,0:T(1,128)S(1)}, f32[32,1,128]{2,1,0:T(1,128)S(1)}, u32[]{:S(2)}, u32[]{:S(2)}) collective-permute-start(f32[32,1,128]{2,1,0:T(1,128)S(1)} %get-tuple-element.52), channel_id=1, source_target_pairs={{16,0},{32,16},{48,32},{64,48},{80,64},{96,80},{112,96},{17,1},{33... | collective-permute-start | bytes 49160 | tf_op jit(solution)/shard_map/ppermute | solution.py:24
  77.7 14.9 %collective-permute-start.4 = (f32[32,1,128]{2,1,0:T(1,128)S(1)}, f32[32,1,128]{2,1,0:T(1,128)S(1)}, u32[]{:S(2)}, u32[]{:S(2)}) collective-permute-start(f32[32,1,128]{2,1,0:T(1,128)S(1)} %get-tuple-element.51), channel_id=1, source_target_pairs={{0,16},{16,32},{32,48},{48,64},{64,80},{80,96},{96,112},{1,17},{17... | collective-permute-start | bytes 49160 | tf_op jit(solution)/shard_map/ppermute | solution.py:23
  81.4 4.5 %collective-permute-start.6 = (f32[1,16,128]{2,1,0:T(8,128)S(1)}, f32[1,16,128]{2,1,0:T(8,128)S(1)}, u32[]{:S(2)}, u32[]{:S(2)}) collective-permute-start(f32[1,16,128]{2,1,0:T(8,128)S(1)} %get-tuple-element.54), channel_id=1, source_target_pairs={{1,0},{2,1},{3,2},{4,3},{5,4},{6,5},{7,6},{8,7},{9,8},{10,9},{11,1... | collective-permute-start | bytes 24584 | tf_op jit(solution)/shard_map/ppermute | solution.py:24
  84.0 8.6 %collective-permute-start.7 = (f32[1,16,128]{2,1,0:T(8,128)S(1)}, f32[1,16,128]{2,1,0:T(8,128)S(1)}, u32[]{:S(2)}, u32[]{:S(2)}) collective-permute-start(f32[1,16,128]{2,1,0:T(8,128)S(1)} %get-tuple-element.53), channel_id=1, source_target_pairs={{0,1},{1,2},{2,3},{3,4},{4,5},{5,6},{6,7},{7,8},{8,9},{9,10},{10,1... | collective-permute-start | bytes 24584 | tf_op jit(solution)/shard_map/ppermute | solution.py:23
  140.7 1.5 copy-start.7
  142.2 4.5 %copy-start = (f32[1,32,128,128]{3,2,1,0:T(8,128)S(1)}, f32[1,32,128,128]{3,2,1,0:T(8,128)}, u32[]{:S(2)}) copy-start(f32[1,32,128,128]{3,2,1,0:T(8,128)} %param.16) | copy-start | bytes 6291460
  142.2 11.0 %copy-start.8 = (f32[1,3]{1,0:T(1,128)S(1)}, f32[1,3]{1,0:T(1,128)}, u32[]{:S(2)}) copy-start(f32[1,3]{1,0:T(1,128)} %param.13) | copy-start | bytes 40
  142.2 30.9 %all-to-all-start = ((f32[8,32,16,128]{3,2,1,0:T(8,128)}), f32[8,32,16,128]{3,2,1,0:T(8,128)}, u32[]{:S(2)}, u32[]{:S(2)}) async-start(f32[8,32,16,128]{3,2,1,0:T(8,128)} %broadcast_in_dim.57), calls=%async_computation | async-start | bytes 4194304 | tf_op jit(solution)/shard_map/all_to_all | solution.py:43
  146.6 34.3 %collective-permute-start.11 = (f32[1,128,128]{2,1,0:T(8,128)S(1)}, f32[1,128,128]{2,1,0:T(8,128)S(1)}, u32[]{:S(2)}, u32[]{:S(2)}) collective-permute-start(f32[1,128,128]{2,1,0:T(8,128)S(1)} %get-tuple-element.48), channel_id=1, source_target_pairs={{1,0},{2,1},{3,2},{4,3},{5,4},{6,5},{7,6},{8,7},{9,8},{10,9},{11,1... | collective-permute-start | bytes 196616 | tf_op jit(solution)/shard_map/ppermute | solution.py:67
  150.0 31.0 %collective-permute-start.10 = (f32[1,128,128]{2,1,0:T(8,128)S(1)}, f32[1,128,128]{2,1,0:T(8,128)S(1)}, u32[]{:S(2)}, u32[]{:S(2)}) collective-permute-start(f32[1,128,128]{2,1,0:T(8,128)S(1)} %get-tuple-element.47), channel_id=1, source_target_pairs={{0,1},{1,2},{2,3},{3,4},{4,5},{5,6},{6,7},{7,8},{8,9},{9,10},{10,1... | collective-permute-start | bytes 196616 | tf_op jit(solution)/shard_map/ppermute | solution.py:65
  173.0 2.2 copy-start.1
  173.0 2.9 copy-start.2
  175.9 9.3 %collective-permute-start.9 = (f32[3,2,128,128]{3,2,1,0:T(8,128)S(1)}, f32[3,2,128,128]{3,2,1,0:T(8,128)S(1)}, u32[]{:S(2)}, u32[]{:S(2)}) collective-permute-start(f32[3,2,128,128]{3,2,1,0:T(8,128)S(1)} %get-tuple-element.44), channel_id=1, source_target_pairs={{1,0},{2,1},{3,2},{4,3},{5,4},{6,5},{7,6},{8,7},{9,8},{10,9},{11,1... | collective-permute-start | bytes 1179656 | tf_op jit(solution)/shard_map/ppermute | solution.py:67
  178.8 12.7 %collective-permute-start.8 = (f32[3,2,128,128]{3,2,1,0:T(8,128)S(1)}, f32[3,2,128,128]{3,2,1,0:T(8,128)S(1)}, u32[]{:S(2)}, u32[]{:S(2)}) collective-permute-start(f32[3,2,128,128]{3,2,1,0:T(8,128)S(1)} %get-tuple-element.43), channel_id=1, source_target_pairs={{0,1},{1,2},{2,3},{3,4},{4,5},{5,6},{6,7},{7,8},{8,9},{9,10},{10,1... | collective-permute-start | bytes 1179656 | tf_op jit(solution)/shard_map/ppermute | solution.py:65
  217.2 15.7 %slice-start = ((s8[4734976]{0:T(1024)(128)(4,1)}), s8[4194304]{0:T(1024)(128)(4,1)S(1)}, s32[]{:S(2)}) async-start(s8[4734976]{0:T(1024)(128)(4,1)} %bitcast.51), calls=%async_computation.1 | async-start | bytes 8388608
  217.2 15.7 %slice-start.2 = ((s8[4734976]{0:T(1024)(128)(4,1)}), s8[4194304]{0:T(1024)(128)(4,1)S(1)}, s32[]{:S(2)}) async-start(s8[4734976]{0:T(1024)(128)(4,1)} %bitcast.53), calls=%async_computation.3 | async-start | bytes 8388608
  217.2 15.7 %slice-start.4 = ((s8[4734976]{0:T(1024)(128)(4,1)}), s8[4194304]{0:T(1024)(128)(4,1)S(1)}, s32[]{:S(2)}) async-start(s8[4734976]{0:T(1024)(128)(4,1)} %bitcast.55), calls=%async_computation.5 | async-start | bytes 8388608
  217.2 15.8 %slice-start.1 = ((s8[4734976]{0:T(1024)(128)(4,1)}), s8[540672]{0:T(1024)(128)(4,1)S(1)}, s32[]{:S(2)}) async-start(s8[4734976]{0:T(1024)(128)(4,1)} %bitcast.51), calls=%async_computation.2 | async-start | bytes 1081344
  217.2 15.8 %slice-start.3 = ((s8[4734976]{0:T(1024)(128)(4,1)}), s8[540672]{0:T(1024)(128)(4,1)S(1)}, s32[]{:S(2)}) async-start(s8[4734976]{0:T(1024)(128)(4,1)} %bitcast.53), calls=%async_computation.4 | async-start | bytes 1081344
  217.2 15.8 %slice-start.5 = ((s8[4734976]{0:T(1024)(128)(4,1)}), s8[540672]{0:T(1024)(128)(4,1)S(1)}, s32[]{:S(2)}) async-start(s8[4734976]{0:T(1024)(128)(4,1)} %bitcast.55), calls=%async_computation.6 | async-start | bytes 1081344
  257.1 4.8 %collective-permute-start.13 = (f32[1,128,128]{2,1,0:T(8,128)S(1)}, f32[1,128,128]{2,1,0:T(8,128)S(1)}, u32[]{:S(2)}, u32[]{:S(2)}) collective-permute-start(f32[1,128,128]{2,1,0:T(8,128)S(1)} %get-tuple-element.46), channel_id=1, source_target_pairs={{1,0},{2,1},{3,2},{4,3},{5,4},{6,5},{7,6},{8,7},{9,8},{10,9},{11,1... | collective-permute-start | bytes 196616 | tf_op jit(solution)/shard_map/ppermute | solution.py:67
  259.0 12.4 %copy-start.3 = (f32[32,128,129]{2,1,0:T(8,128)S(1)}, f32[32,128,129]{2,1,0:T(8,128)}, u32[]{:S(2)}) copy-start(f32[32,128,129]{2,1,0:T(8,128)} %get-tuple-element.32) | copy-start | bytes 6340612
  259.0 9.5 %collective-permute-start.12 = (f32[1,128,128]{2,1,0:T(8,128)S(1)}, f32[1,128,128]{2,1,0:T(8,128)S(1)}, u32[]{:S(2)}, u32[]{:S(2)}) collective-permute-start(f32[1,128,128]{2,1,0:T(8,128)S(1)} %get-tuple-element.45), channel_id=1, source_target_pairs={{0,1},{1,2},{2,3},{3,4},{4,5},{5,6},{6,7},{7,8},{8,9},{9,10},{10,1... | collective-permute-start | bytes 196616 | tf_op jit(solution)/shard_map/ppermute | solution.py:65
  271.4 4.2 %copy-start.4 = (f32[32,129,128]{2,1,0:T(8,128)S(1)}, f32[32,129,128]{2,1,0:T(8,128)}, u32[]{:S(2)}) copy-start(f32[32,129,128]{2,1,0:T(8,128)} %get-tuple-element.30) | copy-start | bytes 6340612
  275.6 1.6 copy-start.5
where the time goes:
time: 286 us; the launch traced here: 285 us
  other arithmetic  109 us (38%)
  blocking collectives  68.7 us (24%)
  starting transfers between devices  44 us (15%)
  waiting for transfers between devices  36.1 us (13%)
  local copies, waits for them, and re-layouts  18.7 us (7%)
  between operations  8.34 us (3%)
    psum x10, blocking collectives, by_axis(): array = lax.psum(array, axis)  68.7 us
    add x6, other arithmetic, transport_step(): jnp.maximum(velocity, 0.0) * conc_low  36.1 us
    concatenate x3, other arithmetic, extended_2(): jnp.concatenate([lax.ppermute(tail, axis, [(i, (i + 1) % count) for i in...  22.5 us
    broadcast_in_dim x2, other arithmetic, local(): return (solution, conc[None], bound[None])  16.9 us
    ppermute x4, waiting for transfers between devices, extended(): lax.ppermute(last, axis, up)  13.3 us
    ppermute x4, starting transfers between devices, extended(): lax.ppermute(initial, axis, [(b, a) for a, b in up])  13 us
    ppermute x3, waiting for transfers between devices, extended_2(): lax.ppermute(tail, axis, [(i, (i + 1) % count) for i in range(ends)])  12.8 us
    ppermute x4, starting transfers between devices, extended(): lax.ppermute(last, axis, up)  11.5 us
  transfers between devices with their start and end apart: 15, of which 5 were waited for; matrix products, arithmetic and copies ran while one was open for 6% of the time, Pallas kernels for 0%

commit v1 on v0

--- a/solution.py
+++ b/solution.py
@@ -34,7 +34,7 @@
 
 def by_axis(array, axes):
     for axis in axes:
-        array = lax.psum(array, axis)
+        array = jnp.sum(lax.all_gather(array, axis), axis=0)
     return array
 
 

time: 286 us -> 318 us (1.11)
  local copies, waits for them, and re-layouts: 18.7 us -> 48.5 us
  other arithmetic: 109 us -> 121 us
  blocking collectives: 68.7 us -> 61.6 us
    psum x10 -> x0, blocking collectives: 68.7 us -> none  [by_axis(): array = lax.psum(array, axis)]
    unnamed x0 -> x10, blocking collectives: none -> 61.6 us
    unnamed x30 -> x83, local copies, waits for them, and re-layouts: 1.28 us -> 31.1 us
    reduce_sum x0 -> x20, other arithmetic: none -> 12.3 us  [by_axis(): array = jnp.sum(lax.all_gather(array, axis), axis=0)]
where the time goes in v1:
time: 318 us; the launch traced here: 317 us
  other arithmetic  121 us (38%)
  blocking collectives  61.6 us (19%)
  local copies, waits for them, and re-layouts  48.5 us (15%)
  starting transfers between devices  44 us (14%)
  waiting for transfers between devices  33.8 us (11%)
  between operations  7.93 us (2%)
    unnamed x10, blocking collectives  61.6 us
    add x6, other arithmetic, transport_step(): jnp.maximum(velocity, 0.0) * conc_low  35.7 us
    unnamed x83, local copies, waits for them, and re-layouts  31.1 us
    concatenate x3, other arithmetic, extended_2(): jnp.concatenate([lax.ppermute(tail, axis, [(i, (i + 1) % count) for i in...  22.5 us
    broadcast_in_dim x2, other arithmetic, local(): return (solution, conc[None], bound[None])  16.9 us
    ppermute x4, starting transfers between devices, extended(): lax.ppermute(initial, axis, [(b, a) for a, b in up])  13 us
    ppermute x3, waiting for transfers between devices, extended_2(): lax.ppermute(tail, axis, [(i, (i + 1) % count) for i in range(ends)])  12.8 us
    reduce_sum x20, other arithmetic, by_axis(): array = jnp.sum(lax.all_gather(array, axis), axis=0)  12.3 us
  transfers between devices with their start and end apart: 15, of which 5 were waited for; matrix products, arithmetic and copies ran while one was open for 6% of the time, Pallas kernels for 0%

profile of v1, /device:TPU:6, one launch (start us, length us, event | category | flops | bytes accessed | tf_op | source)
XLA Modules:
  0.0 316.7 jit_solution(14909029203125427627)
XLA Ops:
  3.5 5.1 %fusion.39 = (f32[32,16,128]{2,1,0:T(8,128)S(1)}, pred[32,16,128]{2,1,0:T(8,128)(4,1)S(1)}, pred[32,16,128]{2,1,0:T(8,128)(4,1)S(1)}) fusion(f32[]{:T(128)} %bitcast.5, f32[]{:T(128)} %bitcast.4, f32[]{:T(128)} %bitcast.3, f32[32,16,128]{2,1,0:T(8,128)} %param.10, f32[]{:T(128)} %bitcast.2, f32[]{:T(128)} %bitcast.1, f32[]{:T(128)} %bitcast, ...), kind=kLoop, calls=%fused_computation.130 | loop fusion | flops 786432 | bytes 917532 | tf_op jit(solution)/shard_map/mul | solution.py:86
  8.6 2.7 collective-permute-start.1
  11.3 4.0 %collective-permute-start = (f32[32,1,128]{2,1,0:T(1,128)S(1)}, f32[32,1,128]{2,1,0:T(1,128)S(1)}, u32[]{:S(2)}, u32[]{:S(2)}) collective-permute-start(f32[32,1,128]{2,1,0:T(1,128)S(1)} %get-tuple-element.55), channel_id=1, source_target_pairs={{0,16},{16,32},{32,48},{48,64},{64,80},{80,96},{96,112},{1,17},{17... | collective-permute-start | bytes 49160 | tf_op jit(solution)/shard_map/ppermute | solution.py:23
  15.4 4.6 %collective-permute-start.2 = (f32[1,16,128]{2,1,0:T(8,128)S(1)}, f32[1,16,128]{2,1,0:T(8,128)S(1)}, u32[]{:S(2)}, u32[]{:S(2)}) collective-permute-start(f32[1,16,128]{2,1,0:T(8,128)S(1)} %get-tuple-element.58), channel_id=1, source_target_pairs={{1,0},{2,1},{3,2},{4,3},{5,4},{6,5},{7,6},{8,7},{9,8},{10,9},{11,1... | collective-permute-start | bytes 24584 | tf_op jit(solution)/shard_map/ppermute | solution.py:24
  20.0 1.9 collective-permute-start.3
  23.2 5.4 %collective-permute-done.3 = f32[1,16,128]{2,1,0:T(8,128)S(1)} collective-permute-done((f32[1,16,128]{2,1,0:T(8,128)S(1)}, f32[1,16,128]{2,1,0:T(8,128)S(1)}, u32[]{:S(2)}, u32[]{:S(2)}) %collective-permute-start.3) | collective-permute-done | bytes 8224 | tf_op jit(solution)/shard_map/ppermute | solution.py:23
  29.1 4.9 %multiply_reduce_fusion.1 = (f32[]{:T(128)}, f32[]{:T(128)}, f32[32,16,128]{2,1,0:T(8,128)S(1)}) fusion(pred[32,16,128]{2,1,0:T(8,128)(4,1)S(1)} %get-tuple-element.39, pred[32,16,128]{2,1,0:T(8,128)(4,1)S(1)} %get-tuple-element.38, f32[]{:T(128)} %bitcast.5, f32[]{:T(128)} %bitcast.4, f32[]{:T(128)} %bitcast.3, f32[32,16,128]{2,1,0:T(8,128)S(1)} %copy-done.6, ...), kind=kLoop, calls=%fused_computation.126 | loop fusion | flops 2031614 | bytes 1493024 | tf_op jit(solution)/shard_map/reduce_sum | solution.py:95
  37.2 9.6 %all-reduce.32 = (f32[4]{0:T(128)S(1)}, f32[4]{0:T(128)S(1)}) all-reduce(f32[4]{0:T(128)S(1)} %dynamic-update-slice, f32[4]{0:T(128)S(1)} %dynamic-update-slice.5), channel_id=1, replica_groups=mesh['size_0'=4,'size_1'=2,'gz_0'=2,'gz_1'=4,'gz_2'=2] {'size_0'}, use_global_device_ids=true, to_apply=%add.9 | all-reduce | flops 8 | bytes 64
  51.5 4.9 %all-reduce.38 = (f32[2]{0:T(128)S(1)}, f32[2]{0:T(128)S(1)}) all-reduce(f32[2]{0:T(128)S(1)} %dynamic-update-slice.1, f32[2]{0:T(128)S(1)} %dynamic-update-slice.6), channel_id=1, replica_groups=mesh['size_0'=4,'size_1'=2,'gz_0'=2,'gz_1'=4,'gz_2'=2] {'size_1'}, use_global_device_ids=true, to_apply=%add.10 | all-reduce | flops 4 | bytes 32
  61.0 6.4 %all-reduce.36 = (f32[2]{0:T(128)S(1)}, f32[2]{0:T(128)S(1)}) all-reduce(f32[2]{0:T(128)S(1)} %dynamic-update-slice.2, f32[2]{0:T(128)S(1)} %dynamic-update-slice.7), channel_id=1, replica_groups=mesh['size_0'=4,'size_1'=2,'gz_0'=2,'gz_1'=4,'gz_2'=2] {'gz_0'}, use_global_device_ids=true, to_apply=%add.11 | all-reduce | flops 4 | bytes 32
  71.8 7.7 %all-reduce.30 = (f32[4]{0:T(128)S(1)}, f32[4]{0:T(128)S(1)}) all-reduce(f32[4]{0:T(128)S(1)} %dynamic-update-slice.3, f32[4]{0:T(128)S(1)} %dynamic-update-slice.8), channel_id=1, replica_groups=mesh['size_0'=4,'size_1'=2,'gz_0'=2,'gz_1'=4,'gz_2'=2] {'gz_1'}, use_global_device_ids=true, to_apply=%add.12 | all-reduce | flops 8 | bytes 64
  83.5 2.4 all-reduce.34
  88.5 4.6 %fusion.38 = (f32[32,16,128]{2,1,0:T(8,128)S(1)}, f32[]{:T(128)}) fusion(pred[32,16,128]{2,1,0:T(8,128)(4,1)S(1)} %get-tuple-element.39, pred[32,16,128]{2,1,0:T(8,128)(4,1)S(1)} %get-tuple-element.38, f32[]{:T(128)} %bitcast.5, f32[]{:T(128)} %bitcast.4, f32[]{:T(128)} %bitcast.3, f32[32,16,128]{2,1,0:T(8,128)S(1)} %get-tuple-element.36, f32[]{:T(128)S(6)} %div.19, ...), kind=kLoop, calls=%fused_computation.129 | loop fusion | flops 917503 | bytes 917536 | tf_op jit(solution)/shard_map/mul | solution.py:86
  93.2 3.0 collective-permute-start.5
  96.2 3.7 %collective-permute-start.4 = (f32[32,1,128]{2,1,0:T(1,128)S(1)}, f32[32,1,128]{2,1,0:T(1,128)S(1)}, u32[]{:S(2)}, u32[]{:S(2)}) collective-permute-start(f32[32,1,128]{2,1,0:T(1,128)S(1)} %get-tuple-element.51), channel_id=1, source_target_pairs={{0,16},{16,32},{32,48},{48,64},{64,80},{80,96},{96,112},{1,17},{17... | collective-permute-start | bytes 49160 | tf_op jit(solution)/shard_map/ppermute | solution.py:23
  99.9 2.5 collective-permute-start.6
  102.5 1.9 collective-permute-start.7
  105.7 5.4 %collective-permute-done.7 = f32[1,16,128]{2,1,0:T(8,128)S(1)} collective-permute-done((f32[1,16,128]{2,1,0:T(8,128)S(1)}, f32[1,16,128]{2,1,0:T(8,128)S(1)}, u32[]{:S(2)}, u32[]{:S(2)}) %collective-permute-start.7) | collective-permute-done | bytes 8224 | tf_op jit(solution)/shard_map/ppermute | solution.py:23
  111.5 4.8 %fusion.28 = f32[]{:T(128)} fusion(f32[34,18,130]{2,1,0:T(8,128)S(1)} %select_maximum_fusion.8, f32[32,16,128]{2,1,0:T(8,128)S(1)} %get-tuple-element.49, f32[32,1,128]{2,1,0:T(1,128)S(1)} %collective-permute-done.4, f32[32,1,128]{2,1,0:T(1,128)S(1)} %collective-permute-done.5, f32[1,18,128]{2,1,0:T(8,128)S(1)} %pad.35, f32[1,18,128]{2,1,0:T(8,128)S(1)} %pad.34, ...), kind=kLoop, calls=%fused_computation.94 | loop fusion | flops 2031615 | bytes 1493024 | tf_op jit(solution)/shard_map/reduce_sum | solution.py:95
  117.6 9.0 %all-reduce.31 = (f32[4]{0:T(128)S(1)}, f32[4]{0:T(128)S(1)}) all-reduce(f32[4]{0:T(128)S(1)} %dynamic-update-slice.10, f32[4]{0:T(128)S(1)} %dynamic-update-slice.15), channel_id=1, replica_groups=mesh['size_0'=4,'size_1'=2,'gz_0'=2,'gz_1'=4,'gz_2'=2] {'size_0'}, use_global_device_ids=true, to_apply=%add.19 | all-reduce | flops 8 | bytes 64
  130.4 4.9 %all-reduce.37 = (f32[2]{0:T(128)S(1)}, f32[2]{0:T(128)S(1)}) all-reduce(f32[2]{0:T(128)S(1)} %dynamic-update-slice.11, f32[2]{0:T(128)S(1)} %dynamic-update-slice.16), channel_id=1, replica_groups=mesh['size_0'=4,'size_1'=2,'gz_0'=2,'gz_1'=4,'gz_2'=2] {'size_1'}, use_global_device_ids=true, to_apply=%add.20 | all-reduce | flops 4 | bytes 32
  139.1 6.4 %all-reduce.35 = (f32[2]{0:T(128)S(1)}, f32[2]{0:T(128)S(1)}) all-reduce(f32[2]{0:T(128)S(1)} %dynamic-update-slice.12, f32[2]{0:T(128)S(1)} %dynamic-update-slice.17), channel_id=1, replica_groups=mesh['size_0'=4,'size_1'=2,'gz_0'=2,'gz_1'=4,'gz_2'=2] {'gz_0'}, use_global_device_ids=true, to_apply=%add.21 | all-reduce | flops 4 | bytes 32
  149.3 7.7 %all-reduce.29 = (f32[4]{0:T(128)S(1)}, f32[4]{0:T(128)S(1)}) all-reduce(f32[4]{0:T(128)S(1)} %dynamic-update-slice.13, f32[4]{0:T(128)S(1)} %dynamic-update-slice.18), channel_id=1, replica_groups=mesh['size_0'=4,'size_1'=2,'gz_0'=2,'gz_1'=4,'gz_2'=2] {'gz_1'}, use_global_device_ids=true, to_apply=%add.22 | all-reduce | flops 8 | bytes 64
  160.7 2.4 all-reduce.33
  168.6 4.0 %multiply_add_fusion.6 = f32[32,16,128]{2,1,0:T(8,128)S(1)} fusion(f32[]{:T(128)S(6)} %div.21, f32[]{:T(128)S(6)} %div.23, f32[]{:T(128)S(6)} %div.19, pred[32,16,128]{2,1,0:T(8,128)(4,1)S(1)} %get-tuple-element.39, pred[32,16,128]{2,1,0:T(8,128)(4,1)S(1)} %get-tuple-element.38, f32[]{:T(128)} %bitcast.5, f32[]{:T(128)} %bitcast.4, f32[]{:T(128)} %bitcast.3, ...), kind=kLoop, calls=%fused_computation.123 | loop fusion | flops 1114112 | bytes 917540 | tf_op jit(solution)/shard_map/add | solution.py:169
  174.2 4.4 %all-to-all-start = ((f32[8,32,16,128]{3,2,1,0:T(8,128)}), f32[8,32,16,128]{3,2,1,0:T(8,128)}, u32[]{:S(2)}, u32[]{:S(2)}) async-start(f32[8,32,16,128]{3,2,1,0:T(8,128)} %broadcast_in_dim.57), calls=%async_computation | async-start | bytes 4194304 | tf_op jit(solution)/shard_map/all_to_all | solution.py:43
  178.6 3.3 %collective-permute-start.11 = (f32[1,128,128]{2,1,0:T(8,128)S(1)}, f32[1,128,128]{2,1,0:T(8,128)S(1)}, u32[]{:S(2)}, u32[]{:S(2)}) collective-permute-start(f32[1,128,128]{2,1,0:T(8,128)S(1)} %get-tuple-element.48), channel_id=1, source_target_pairs={{1,0},{2,1},{3,2},{4,3},{5,4},{6,5},{7,6},{8,7},{9,8},{10,9},{11,1... | collective-permute-start | bytes 196616 | tf_op jit(solution)/shard_map/ppermute | solution.py:67
  182.0 1.9 collective-permute-start.10
  185.8 5.5 %select_bitcast_fusion.1 = (f32[1,32,128,128]{3,2,1,0:T(8,128)}, pred[32,128,128]{2,1,0:T(8,128)(4,1)S(1)}, pred[32,128,128]{2,1,0:T(8,128)(4,1)S(1)}) fusion(f32[]{:T(128)} %bitcast.5, f32[]{:T(128)} %bitcast.4, f32[]{:T(128)} %bitcast.3, s32[32,128,128]{2,1,0:T(8,128)} %param.9), kind=kLoop, calls=%fused_computation.68 | loop fusion | flops 2097152 | bytes 5242892 | tf_op jit(solution)/shard_map/stack | solution.py:183
  191.3 3.5 %select_bitcast_fusion = f32[1,32,128,128]{3,2,1,0:T(8,128)} fusion(pred[32,128,128]{2,1,0:T(8,128)(4,1)S(1)} %get-tuple-element.35, pred[32,128,128]{2,1,0:T(8,128)(4,1)S(1)} %get-tuple-element.34, f32[]{:T(128)} %bitcast.38, f32[]{:T(128)} %bitcast.37, f32[]{:T(128)} %bitcast.36), kind=kLoop, calls=%fused_computation.67 | loop fusion | flops 1048576 | bytes 3145740 | tf_op jit(solution)/shard_map/stack | solution.py:183
  194.8 10.2 %all-to-all-done = f32[8,32,16,128]{3,2,1,0:T(8,128)} async-done(((f32[8,32,16,128]{3,2,1,0:T(8,128)}), f32[8,32,16,128]{3,2,1,0:T(8,128)}, u32[]{:S(2)}, u32[]{:S(2)}) %all-to-all-start) | async-done | bytes 2097184 | tf_op jit(solution)/shard_map/all_to_all | solution.py:43
  205.0 2.0 copy.12
  207.9 2.9 collective-permute-start.9
  210.8 2.1 collective-permute-start.8
  213.0 4.3 %select_maximum_fusion.6 = f32[34,130,130]{2,1,0:T(8,128)} fusion(f32[1,128,128]{2,1,0:T(8,128)S(1)} %collective-permute-done.11, f32[32,128,128]{2,1,0:T(8,128)S(1)} %bitcast.82, f32[1,128,128]{2,1,0:T(8,128)S(1)} %collective-permute-done.10), kind=kLoop, calls=%fused_computation.18 | loop fusion | flops 8619000 | bytes 4526624 | tf_op jit(solution)/shard_map/concatenate | solution.py:63
  217.3 6.3 %collective-permute-done.8 = f32[3,2,128,128]{3,2,1,0:T(8,128)S(1)} collective-permute-done((f32[3,2,128,128]{3,2,1,0:T(8,128)S(1)}, f32[3,2,128,128]{3,2,1,0:T(8,128)S(1)}, u32[]{:S(2)}, u32[]{:S(2)}) %collective-permute-start.8) | collective-permute-done | bytes 393248 | tf_op jit(solution)/shard_map/ppermute | solution.py:65
  223.5 15.3 %select_maximum_fusion = f32[3,36,130,130]{3,2,1,0:T(8,128)} fusion(f32[3,2,128,128]{3,2,1,0:T(8,128)S(1)} %collective-permute-done.9, f32[3,2,128,128]{3,2,1,0:T(8,128)S(1)} %collective-permute-done.8, f32[1,32,128,128]{3,2,1,0:T(8,128)S(1)} %copy-done.2, f32[1,32,128,128]{3,2,1,0:T(8,128)S(1)} %copy-done.1, f32[1,32,128,128]{3,2,1,0:T(8,128)S(1)} %bitcast.85), kind=kLoop, calls=%fused_computation.4 | loop fusion | flops 38329200 | bytes 14378688 | tf_op jit(solution)/shard_map/concatenate | solution.py:63
  238.9 10.4 %slice_bitcast_fusion.2 = (f32[34,130,130]{2,1,0:T(8,128)}, f32[34,130,130]{2,1,0:T(8,128)}, f32[34,130,130]{2,1,0:T(8,128)}) fusion(f32[3,36,130,130]{3,2,1,0:T(8,128)} %select_maximum_fusion), kind=kLoop, calls=%fused_computation.21 | loop fusion | bytes 13790400 | tf_op jit(solution)/shard_map/squeeze | solution.py:116
  249.3 15.4 %multiply_add_fusion.1 = (f32[32,128,129]{2,1,0:T(8,128)}, f32[32,128,129]{2,1,0:T(8,128)}) fusion(f32[34,130,130]{2,1,0:T(8,128)} %select_maximum_fusion.6, f32[]{:T(128)} %bitcast.72, f32[34,130,130]{2,1,0:T(8,128)} %get-tuple-element.41, f32[34,130,130]{2,1,0:T(8,128)} %get-tuple-element.40, f32[]{:T(128)} %bitcast.69), kind=kLoop, calls=%fused_computation.30 | loop fusion | flops 6340608 | bytes 16908296 | tf_op jit(solution)/shard_map/add | solution.py:126
  264.8 5.0 %multiply_add_fusion.3 = (f32[32,129,128]{2,1,0:T(8,128)}, f32[32,129,128]{2,1,0:T(8,128)}) fusion(f32[34,130,130]{2,1,0:T(8,128)S(1)} %bitcast.81, f32[]{:T(128)} %bitcast.71, f32[34,130,130]{2,1,0:T(8,128)S(1)} %bitcast.79, f32[34,130,130]{2,1,0:T(8,128)S(1)} %bitcast.77, f32[]{:T(128)} %bitcast.68), kind=kLoop, calls=%fused_computation.36 | loop fusion | flops 6340608 | bytes 16908296 | tf_op jit(solution)/shard_map/add | solution.py:126
  269.7 9.3 %multiply_add_fusion.5 = (f32[33,128,128]{2,1,0:T(8,128)}, f32[33,128,128]{2,1,0:T(8,128)}) fusion(f32[1,128,128]{2,1,0:T(8,128)S(1)} %collective-permute-done.11, f32[32,128,128]{2,1,0:T(8,128)S(1)} %bitcast.83, f32[1,128,128]{2,1,0:T(8,128)S(1)} %collective-permute-done.10, f32[]{:T(128)} %bitcast.70, f32[34,130,130]{2,1,0:T(8,128)} %get-tuple-element.41, ...), kind=kLoop, calls=%fused_computation.46 | loop fusion | flops 7569408 | bytes 15204360 | tf_op jit(solution)/shard_map/add | solution.py:126
  279.1 9.6 %fusion.21 = (f32[1,32,128,128]{3,2,1,0:T(8,128)}, f32[32,128,128]{2,1,0:T(8,128)S(1)}) fusion(f32[1,32,128,128]{3,2,1,0:T(8,128)} %param.17, f32[34,130,130]{2,1,0:T(8,128)} %get-tuple-element.42, f32[1,32,128,128]{3,2,1,0:T(8,128)S(1)} %copy-done, f32[32,128,129]{2,1,0:T(8,128)} %get-tuple-element.31, f32[32,129,128]{2,1,0:T(8,128)} %get-tuple-element.29, ...), kind=kLoop, calls=%fused_computation.66 | loop fusion | flops 7340032 | bytes 23068672 | tf_op jit(solution)/shard_map/broadcast_in_dim | solution.py:195
  288.7 1.9 collective-permute-start.13
  290.6 2.9 collective-permute-start.12
  293.5 6.6 %collective-permute-done.12 = f32[1,128,128]{2,1,0:T(8,128)S(1)} collective-permute-done((f32[1,128,128]{2,1,0:T(8,128)S(1)}, f32[1,128,128]{2,1,0:T(8,128)S(1)}, u32[]{:S(2)}, u32[]{:S(2)}) %collective-permute-start.12) | collective-permute-done | bytes 65568 | tf_op jit(solution)/shard_map/ppermute | solution.py:65
  300.1 2.9 select_maximum_fusion.4
  303.0 4.2 %multiply_add_fusion = f32[32,128,129]{2,1,0:T(8,128)} fusion(f32[34,130,130]{2,1,0:T(8,128)S(1)} %select_maximum_fusion.4, f32[32,128,129]{2,1,0:T(8,128)S(1)} %copy-done.3, f32[]{:T(128)} %bitcast.73), kind=kLoop, calls=%fused_computation.29 | loop fusion | flops 4227072 | bytes 8454148 | tf_op jit(solution)/shard_map/add | solution.py:126
  309.5 7.3 %fusion.13 = f32[1,32,128,128]{3,2,1,0:T(8,128)} fusion(f32[32,128,128]{2,1,0:T(8,128)S(1)} %get-tuple-element.26, f32[32,128,129]{2,1,0:T(8,128)} %multiply_add_fusion, f32[32,129,128]{2,1,0:T(8,128)S(1)} %multiply_add_fusion.2, f32[33,128,128]{2,1,0:T(8,128)S(1)} %multiply_add_fusion.4, f32[34,130,130]{2,1,0:T(8,128)} %get-tuple-element.42), kind=kLoop, calls=%fused_computation.52 | loop fusion | flops 4718592 | bytes 18874368 | tf_op jit(solution)/shard_map/broadcast_in_dim | solution.py:195
  (135 shorter events, 51.2 us)
Async XLA Ops:
  0.6 35.9 %copy-start.12 = (u32[128]{0:T(128)S(1)}, u32[128]{0:T(128)}, u32[]{:S(2)}) copy-start(u32[128]{0:T(128)} %constant.65) | copy-start | bytes 1540
  0.6 50.2 %copy-start.11 = (u32[128]{0:T(128)S(1)}, u32[128]{0:T(128)}, u32[]{:S(2)}) copy-start(u32[128]{0:T(128)} %constant.70) | copy-start | bytes 1540
  0.7 59.7 %copy-start.10 = (u32[128]{0:T(128)S(1)}, u32[128]{0:T(128)}, u32[]{:S(2)}) copy-start(u32[128]{0:T(128)} %constant.75) | copy-start | bytes 1540
  0.7 70.6 %copy-start.9 = (u32[128]{0:T(128)S(1)}, u32[128]{0:T(128)}, u32[]{:S(2)}) copy-start(u32[128]{0:T(128)} %constant.80) | copy-start | bytes 1540
  0.7 28.4 %copy-start.6 = (f32[32,16,128]{2,1,0:T(8,128)S(1)}, f32[32,16,128]{2,1,0:T(8,128)}, u32[]{:S(2)}) copy-start(f32[32,16,128]{2,1,0:T(8,128)} %param.10) | copy-start | bytes 786436
  8.6 20.0 %collective-permute-start.1 = (f32[32,1,128]{2,1,0:T(1,128)S(1)}, f32[32,1,128]{2,1,0:T(1,128)S(1)}, u32[]{:S(2)}, u32[]{:S(2)}) collective-permute-start(f32[32,1,128]{2,1,0:T(1,128)S(1)} %get-tuple-element.56), channel_id=1, source_target_pairs={{16,0},{32,16},{48,32},{64,48},{80,64},{96,80},{112,96},{17,1},{33... | collective-permute-start | bytes 49160 | tf_op jit(solution)/shard_map/ppermute | solution.py:24
  11.3 17.3 %collective-permute-start = (f32[32,1,128]{2,1,0:T(1,128)S(1)}, f32[32,1,128]{2,1,0:T(1,128)S(1)}, u32[]{:S(2)}, u32[]{:S(2)}) collective-permute-start(f32[32,1,128]{2,1,0:T(1,128)S(1)} %get-tuple-element.55), channel_id=1, source_target_pairs={{0,16},{16,32},{32,48},{48,64},{64,80},{80,96},{96,112},{1,17},{17... | collective-permute-start | bytes 49160 | tf_op jit(solution)/shard_map/ppermute | solution.py:23
  15.4 7.8 %collective-permute-start.2 = (f32[1,16,128]{2,1,0:T(8,128)S(1)}, f32[1,16,128]{2,1,0:T(8,128)S(1)}, u32[]{:S(2)}, u32[]{:S(2)}) collective-permute-start(f32[1,16,128]{2,1,0:T(8,128)S(1)} %get-tuple-element.58), channel_id=1, source_target_pairs={{1,0},{2,1},{3,2},{4,3},{5,4},{6,5},{7,6},{8,7},{9,8},{10,9},{11,1... | collective-permute-start | bytes 24584 | tf_op jit(solution)/shard_map/ppermute | solution.py:24
  20.0 8.6 %collective-permute-start.3 = (f32[1,16,128]{2,1,0:T(8,128)S(1)}, f32[1,16,128]{2,1,0:T(8,128)S(1)}, u32[]{:S(2)}, u32[]{:S(2)}) collective-permute-start(f32[1,16,128]{2,1,0:T(8,128)S(1)} %get-tuple-element.57), channel_id=1, source_target_pairs={{0,1},{1,2},{2,3},{3,4},{4,5},{5,6},{6,7},{7,8},{8,9},{9,10},{10,1... | collective-permute-start | bytes 24584 | tf_op jit(solution)/shard_map/ppermute | solution.py:23
  93.2 17.9 %collective-permute-start.5 = (f32[32,1,128]{2,1,0:T(1,128)S(1)}, f32[32,1,128]{2,1,0:T(1,128)S(1)}, u32[]{:S(2)}, u32[]{:S(2)}) collective-permute-start(f32[32,1,128]{2,1,0:T(1,128)S(1)} %get-tuple-element.52), channel_id=1, source_target_pairs={{16,0},{32,16},{48,32},{64,48},{80,64},{96,80},{112,96},{17,1},{33... | collective-permute-start | bytes 49160 | tf_op jit(solution)/shard_map/ppermute | solution.py:24
  96.2 14.9 %collective-permute-start.4 = (f32[32,1,128]{2,1,0:T(1,128)S(1)}, f32[32,1,128]{2,1,0:T(1,128)S(1)}, u32[]{:S(2)}, u32[]{:S(2)}) collective-permute-start(f32[32,1,128]{2,1,0:T(1,128)S(1)} %get-tuple-element.51), channel_id=1, source_target_pairs={{0,16},{16,32},{32,48},{48,64},{64,80},{80,96},{96,112},{1,17},{17... | collective-permute-start | bytes 49160 | tf_op jit(solution)/shard_map/ppermute | solution.py:23
  99.9 5.7 %collective-permute-start.6 = (f32[1,16,128]{2,1,0:T(8,128)S(1)}, f32[1,16,128]{2,1,0:T(8,128)S(1)}, u32[]{:S(2)}, u32[]{:S(2)}) collective-permute-start(f32[1,16,128]{2,1,0:T(8,128)S(1)} %get-tuple-element.54), channel_id=1, source_target_pairs={{1,0},{2,1},{3,2},{4,3},{5,4},{6,5},{7,6},{8,7},{9,8},{10,9},{11,1... | collective-permute-start | bytes 24584 | tf_op jit(solution)/shard_map/ppermute | solution.py:24
  102.5 8.6 %collective-permute-start.7 = (f32[1,16,128]{2,1,0:T(8,128)S(1)}, f32[1,16,128]{2,1,0:T(8,128)S(1)}, u32[]{:S(2)}, u32[]{:S(2)}) collective-permute-start(f32[1,16,128]{2,1,0:T(8,128)S(1)} %get-tuple-element.53), channel_id=1, source_target_pairs={{0,1},{1,2},{2,3},{3,4},{4,5},{5,6},{6,7},{7,8},{8,9},{9,10},{10,1... | collective-permute-start | bytes 24584 | tf_op jit(solution)/shard_map/ppermute | solution.py:23
  172.7 1.5 copy-start.7
  174.2 4.4 %copy-start = (f32[1,32,128,128]{3,2,1,0:T(8,128)S(1)}, f32[1,32,128,128]{3,2,1,0:T(8,128)}, u32[]{:S(2)}) copy-start(f32[1,32,128,128]{3,2,1,0:T(8,128)} %param.16) | copy-start | bytes 6291460
  174.2 11.0 %copy-start.8 = (f32[1,3]{1,0:T(1,128)S(1)}, f32[1,3]{1,0:T(1,128)}, u32[]{:S(2)}) copy-start(f32[1,3]{1,0:T(1,128)} %param.13) | copy-start | bytes 40
  174.2 30.8 %all-to-all-start = ((f32[8,32,16,128]{3,2,1,0:T(8,128)}), f32[8,32,16,128]{3,2,1,0:T(8,128)}, u32[]{:S(2)}, u32[]{:S(2)}) async-start(f32[8,32,16,128]{3,2,1,0:T(8,128)} %broadcast_in_dim.57), calls=%async_computation | async-start | bytes 4194304 | tf_op jit(solution)/shard_map/all_to_all | solution.py:43
  178.6 34.3 %collective-permute-start.11 = (f32[1,128,128]{2,1,0:T(8,128)S(1)}, f32[1,128,128]{2,1,0:T(8,128)S(1)}, u32[]{:S(2)}, u32[]{:S(2)}) collective-permute-start(f32[1,128,128]{2,1,0:T(8,128)S(1)} %get-tuple-element.48), channel_id=1, source_target_pairs={{1,0},{2,1},{3,2},{4,3},{5,4},{6,5},{7,6},{8,7},{9,8},{10,9},{11,1... | collective-permute-start | bytes 196616 | tf_op jit(solution)/shard_map/ppermute | solution.py:67
  182.0 31.0 %collective-permute-start.10 = (f32[1,128,128]{2,1,0:T(8,128)S(1)}, f32[1,128,128]{2,1,0:T(8,128)S(1)}, u32[]{:S(2)}, u32[]{:S(2)}) collective-permute-start(f32[1,128,128]{2,1,0:T(8,128)S(1)} %get-tuple-element.47), channel_id=1, source_target_pairs={{0,1},{1,2},{2,3},{3,4},{4,5},{5,6},{6,7},{7,8},{8,9},{9,10},{10,1... | collective-permute-start | bytes 196616 | tf_op jit(solution)/shard_map/ppermute | solution.py:65
  205.0 2.2 copy-start.1
  205.0 2.9 copy-start.2
  207.9 9.3 %collective-permute-start.9 = (f32[3,2,128,128]{3,2,1,0:T(8,128)S(1)}, f32[3,2,128,128]{3,2,1,0:T(8,128)S(1)}, u32[]{:S(2)}, u32[]{:S(2)}) collective-permute-start(f32[3,2,128,128]{3,2,1,0:T(8,128)S(1)} %get-tuple-element.44), channel_id=1, source_target_pairs={{1,0},{2,1},{3,2},{4,3},{5,4},{6,5},{7,6},{8,7},{9,8},{10,9},{11,1... | collective-permute-start | bytes 1179656 | tf_op jit(solution)/shard_map/ppermute | solution.py:67
  210.8 12.7 %collective-permute-start.8 = (f32[3,2,128,128]{3,2,1,0:T(8,128)S(1)}, f32[3,2,128,128]{3,2,1,0:T(8,128)S(1)}, u32[]{:S(2)}, u32[]{:S(2)}) collective-permute-start(f32[3,2,128,128]{3,2,1,0:T(8,128)S(1)} %get-tuple-element.43), channel_id=1, source_target_pairs={{0,1},{1,2},{2,3},{3,4},{4,5},{5,6},{6,7},{7,8},{8,9},{9,10},{10,1... | collective-permute-start | bytes 1179656 | tf_op jit(solution)/shard_map/ppermute | solution.py:65
  249.3 15.4 %slice-start = ((s8[4734976]{0:T(1024)(128)(4,1)}), s8[4194304]{0:T(1024)(128)(4,1)S(1)}, s32[]{:S(2)}) async-start(s8[4734976]{0:T(1024)(128)(4,1)} %bitcast.76), calls=%async_computation.1 | async-start | bytes 8388608
  249.3 15.4 %slice-start.2 = ((s8[4734976]{0:T(1024)(128)(4,1)}), s8[4194304]{0:T(1024)(128)(4,1)S(1)}, s32[]{:S(2)}) async-start(s8[4734976]{0:T(1024)(128)(4,1)} %bitcast.78), calls=%async_computation.3 | async-start | bytes 8388608
  249.3 15.4 %slice-start.4 = ((s8[4734976]{0:T(1024)(128)(4,1)}), s8[4194304]{0:T(1024)(128)(4,1)S(1)}, s32[]{:S(2)}) async-start(s8[4734976]{0:T(1024)(128)(4,1)} %bitcast.80), calls=%async_computation.5 | async-start | bytes 8388608
  249.3 15.4 %slice-start.1 = ((s8[4734976]{0:T(1024)(128)(4,1)}), s8[540672]{0:T(1024)(128)(4,1)S(1)}, s32[]{:S(2)}) async-start(s8[4734976]{0:T(1024)(128)(4,1)} %bitcast.76), calls=%async_computation.2 | async-start | bytes 1081344
  249.3 15.4 %slice-start.3 = ((s8[4734976]{0:T(1024)(128)(4,1)}), s8[540672]{0:T(1024)(128)(4,1)S(1)}, s32[]{:S(2)}) async-start(s8[4734976]{0:T(1024)(128)(4,1)} %bitcast.78), calls=%async_computation.4 | async-start | bytes 1081344
  249.3 15.4 %slice-start.5 = ((s8[4734976]{0:T(1024)(128)(4,1)}), s8[540672]{0:T(1024)(128)(4,1)S(1)}, s32[]{:S(2)}) async-start(s8[4734976]{0:T(1024)(128)(4,1)} %bitcast.80), calls=%async_computation.6 | async-start | bytes 1081344
  288.7 4.8 %collective-permute-start.13 = (f32[1,128,128]{2,1,0:T(8,128)S(1)}, f32[1,128,128]{2,1,0:T(8,128)S(1)}, u32[]{:S(2)}, u32[]{:S(2)}) collective-permute-start(f32[1,128,128]{2,1,0:T(8,128)S(1)} %get-tuple-element.46), channel_id=1, source_target_pairs={{1,0},{2,1},{3,2},{4,3},{5,4},{6,5},{7,6},{8,7},{9,8},{10,9},{11,1... | collective-permute-start | bytes 196616 | tf_op jit(solution)/shard_map/ppermute | solution.py:67
  290.6 12.4 %copy-start.3 = (f32[32,128,129]{2,1,0:T(8,128)S(1)}, f32[32,128,129]{2,1,0:T(8,128)}, u32[]{:S(2)}) copy-start(f32[32,128,129]{2,1,0:T(8,128)} %get-tuple-element.32) | copy-start | bytes 6340612
  290.6 9.5 %collective-permute-start.12 = (f32[1,128,128]{2,1,0:T(8,128)S(1)}, f32[1,128,128]{2,1,0:T(8,128)S(1)}, u32[]{:S(2)}, u32[]{:S(2)}) collective-permute-start(f32[1,128,128]{2,1,0:T(8,128)S(1)} %get-tuple-element.45), channel_id=1, source_target_pairs={{0,1},{1,2},{2,3},{3,4},{4,5},{5,6},{6,7},{7,8},{8,9},{9,10},{10,1... | collective-permute-start | bytes 196616 | tf_op jit(solution)/shard_map/ppermute | solution.py:65
  303.0 4.2 %copy-start.4 = (f32[32,129,128]{2,1,0:T(8,128)S(1)}, f32[32,129,128]{2,1,0:T(8,128)}, u32[]{:S(2)}) copy-start(f32[32,129,128]{2,1,0:T(8,128)} %get-tuple-element.30) | copy-start | bytes 6340612
  307.2 1.6 copy-start.5
